TPU v7x, 32 devices: a whole 2x2x4 slice. The times are simulated.
32 devices in a mesh: ref: 2 (over y), dat: 16 (over z, x, core).
Axes of the slice: x: 2, y: 2, z: 4, core: 2. Of those that a mesh axis runs over, the one named last changes fastest.
Arguments:
- particles: bfloat16 [1024, 16384], P('dat'), may hold values from -64 to 64
- references: bfloat16 [2, 72, 16384], P(None, 'ref'), may hold values from -0.046875 to 0.046875
- normalizers: float32 [2, 72], P(None, 'ref'), may hold values from 0 to 3
- class_order: int32 [2], replicated, may hold values from 0 to 1, each once
- shift_offsets: int32 [9, 2], replicated, may hold values from -4 to 4, as said below
Outputs:
- class_sums: float32 [2, 72, 16384], P(None, 'ref', 'dat')
- evidence: float32 [2, 1024], P(None, 'dat')
Inputs may be any that keep to these rules, and one draw needn't show every extreme that they name: `shift_offsets`: the nine offset pairs are the grid the finite set (-4, 0, 4) x the finite set (-s, 0, s) for some s of 1 to 4, row offset first; all pairs differ.
All inputs are finite; a program needn't handle non-finite values.
Results may differ from a plain program's by a relative error of at most 0.0027.
Values sent between devices are 32-bit elements; how exact they have to be, the bound alone decides.
A program may use at most 128 MiB of HBM per device.

v0:
```python
import math

import jax
import jax.numpy as jnp
from jax import lax
from jax.sharding import PartitionSpec as P

SIDE = 128
ROT = 72
SHIFTS = 9
CLASSES = 2


def shifted_table(class_refs, shift_offsets):
    local_rots = class_refs.shape[0]
    images = class_refs.reshape(local_rots, SIDE, SIDE)
    moved_refs = [
        jnp.roll(
            images, (shift_offsets[shift_index, 0], shift_offsets[shift_index, 1]), axis=(1, 2)
        )
        for shift_index in range(SHIFTS)
    ]
    return jnp.stack(moved_refs, axis=1).reshape(local_rots * SHIFTS, SIDE * SIDE)


def align_back(weighted, shift_offsets):
    weighted_grids = weighted.reshape(-1, SHIFTS, SIDE, SIDE)
    result = jnp.zeros((weighted_grids.shape[0], SIDE, SIDE), jnp.float32)
    for shift_index in range(SHIFTS):
        result = result + jnp.roll(
            weighted_grids[:, shift_index],
            (-shift_offsets[shift_index, 0], -shift_offsets[shift_index, 1]),
            axis=(1, 2),
        )
    return result.reshape(weighted_grids.shape[0], SIDE * SIDE)


def per_device(particles, references, normalizers, class_order, shift_offsets):
    local_count = particles.shape[0]
    norm_scale = float(ROT) / math.sqrt(local_count * lax.axis_size("dat"))
    partials = []
    evidence = []
    for step_index in range(CLASSES):
        chosen = class_order[step_index]
        class_refs = lax.dynamic_index_in_dim(references, chosen, 0, keepdims=False)
        norm_row = lax.dynamic_index_in_dim(normalizers, chosen, 0, keepdims=False)
        shift_table = shifted_table(class_refs, shift_offsets)
        scores = lax.dot_general(
            particles, shift_table, (((1,), (1,)), ((), ())), preferred_element_type=jnp.float32
        )
        scores = scores.reshape(local_count, class_refs.shape[0], SHIFTS) - norm_row[None, :, None]
        local_high = jnp.max(scores, axis=(1, 2))
        highest = lax.pmax(local_high, "ref")
        shifted_exp = jnp.exp(scores - highest[:, None, None])
        partition = lax.psum(jnp.sum(shifted_exp, axis=(1, 2)), "ref")
        weights = (
            (shifted_exp / partition[:, None, None]).astype(jnp.bfloat16).reshape(local_count, -1)
        )
        weighted = lax.dot_general(
            weights, particles, (((0,), (0,)), ((), ())), preferred_element_type=jnp.float32
        )
        partials.append(align_back(weighted, shift_offsets) * norm_scale)
        evidence.append(highest + jnp.log(partition))
    class_sums = jnp.stack(
        [
            lax.psum_scatter(partial_sum, "dat", scatter_dimension=1, tiled=True)
            for partial_sum in partials
        ]
    )
    return (class_sums, jnp.stack(evidence))


def solution(mesh):
    return jax.shard_map(
        per_device,
        mesh=mesh,
        in_specs=(P("dat", None), P(None, "ref", None), P(None, "ref"), P(), P()),
        out_specs=(P(None, "ref", "dat"), P(None, "dat")),
        check_vma=False,
    )
```

profile of v0, /device:TPU:0, one launch (start us, length us, event | category | flops | bytes accessed | tf_op | source)
XLA Modules:
  0.0 420.7 jit_solution(3708016316304876656)
XLA Ops:
  7.2 1.4 fusion.119
  11.3 2.0 fusion.118
  60.9 15.9 %dynamic-slice_reduce_fusion.1 = (bf16[36,16384]{1,0:T(8,128)(2,1)S(1)}, bf16[36,16384]{1,0:T(8,128)(2,1)S(1)}) fusion(bf16[2,36,16384]{2,0,1:T(2,128)(2,1)} %param.10, s32[]{:T(128)S(6)} %select_n.41, s32[]{:T(128)S(6)} %select_n.42), kind=kLoop, calls=%fused_computation.181 | loop fusion | bytes 4718600 | tf_op jit(solution)/shard_map/jit(dynamic_index_in_dim)/dynamic_slice | solution.py:45
  82.6 13.6 %constant_dynamic-slice_fusion.8 = (bf16[36,128,128]{2,1,0:T(8,128)(2,1)S(1)}, bf16[36,128,128]{2,1,0:T(8,128)(2,1)}, bf16[36,128,128]{2,1,0:T(8,128)(2,1)}, bf1...) fusion(bf16[36,256,128]{2,1,0:T(8,128)(2,1)} %slice_dynamic-upd, ...), kind=kLoop, calls=%fused_computation.264 | loop fusion | bytes 21233700 | tf_op jit(solution)/shard_map/jit(_roll_dynamic)/dynamic_slice | solution.py:18
  96.2 13.0 %constant_dynamic-slice_fusion.3 = (bf16[36,128,128]{2,1,0:T(8,128)(2,1)}, bf16[36,128,128]{2,1,0:T(8,128)(2,1)}, bf16[36,128,128]{2,1,0:T(8,128)(2,1)}, bf16[36...) fusion(bf16[36,256,128]{2,1,0:T(8,128)(2,1)} %slice_dynamic-upd, ...), kind=kLoop, calls=%fused_computation.259 | loop fusion | bytes 21233700 | tf_op jit(solution)/shard_map/jit(_roll_dynamic)/dynamic_slice | solution.py:18
  109.2 2.9 fusion.84
  124.3 7.8 %copy.31 = bf16[41,8,128,128]{3,1,2,0:T(8,128)(2,1)S(1)} copy(bf16[41,8,128,128]{3,2,1,0:T(8,128)(2,1)S(1)} %bitcast.346) | data formatting | bytes 21495808
  144.3 1.8 pad.112
  146.0 7.6 %copy.28 = bf16[41,8,128,128]{3,1,2,0:T(8,128)(2,1)S(1)} copy(bf16[41,8,128,128]{3,2,1,0:T(8,128)(2,1)S(1)} %bitcast.345) | data formatting | bytes 21495808
  153.7 3.4 fusion.120
  157.0 3.4 fusion.121
  160.4 5.9 %all-reduce.1 = (f32[64]{0:T(128)S(1)}, f32[64]{0:T(128)S(1)}) all-reduce(f32[64]{0:T(128)S(1)} %get-tuple-element.70, f32[64]{0:T(128)S(1)} %get-tuple-element.72), channel_id=1, replica_groups=mesh['ref'=2,'dat'=16] {'ref'}, use_global_device_ids=true, to_apply=%region_6.9 | all-reduce | flops 128 | bytes 1024 | tf_op jit(solution)/shard_map/pmax | solution.py:53
  166.6 4.9 %all-reduce = (f32[64]{0:T(128)S(1)}, f32[64]{0:T(128)S(1)}) all-reduce(f32[64]{0:T(128)S(1)} %fusion.115, f32[64]{0:T(128)S(1)} %fusion.114), channel_id=1, replica_groups=mesh['ref'=2,'dat'=16] {'ref'}, use_global_device_ids=true, to_apply=%region_8.11 | all-reduce | flops 128 | bytes 1024 | tf_op jit(solution)/shard_map/psum | solution.py:55
  172.1 9.5 %fusion.54 = f32[36,9,128,128]{3,0,2,1:T(8,128)} fusion(bf16[36,9,64,1]{2,1,0,3:T(8,128)(2,1)S(1)} %bitcast.360, bf16[64,16384]{1,0:T(8,128)(2,1)S(1)} %copy-done), kind=kOutput, calls=%fused_computation.183 | convolution fusion | flops 679477248 | bytes 23372288 | tf_op jit(solution)/shard_map/dot_general | solution.py:59
  181.7 16.2 %slice_bitcast_fusion.8 = (f32[36,128,128]{2,0,1:T(8,128)}, f32[36,128,128]{2,0,1:T(8,128)}, f32[36,128,128]{2,0,1:T(8,128)}, f32[36,128,128]{2,0,1:T(8,128)}, f...) fusion(f32[36,9,128,128]{3,0,2,1:T(8,128)} %fusion.54), kind=kLoop, calls=%fused_computation.134 | loop fusion | bytes 42467328 | tf_op jit(solution)/shard_map/squeeze | solution.py:31
  197.9 9.5 %fusion.55 = f32[36,9,128,128]{3,0,2,1:T(8,128)} fusion(bf16[36,9,64,1]{2,1,0,3:T(8,128)(2,1)S(1)} %bitcast.359, bf16[64,16384]{1,0:T(8,128)(2,1)S(1)} %copy-done), kind=kOutput, calls=%fused_computation.184 | convolution fusion | flops 679477248 | bytes 23372288 | tf_op jit(solution)/shard_map/dot_general | solution.py:59
  207.4 16.5 %slice_bitcast_fusion.17 = (f32[36,128,128]{2,0,1:T(8,128)}, f32[36,128,128]{2,0,1:T(8,128)}, f32[36,128,128]{2,0,1:T(8,128)}, f32[36,128,128]{2,0,1:T(8,128)}, ...) fusion(f32[36,9,128,128]{3,0,2,1:T(8,128)} %fusion.55), kind=kLoop, calls=%fused_computation.143 | loop fusion | bytes 42467328 | tf_op jit(solution)/shard_map/squeeze | solution.py:31
  224.1 6.0 %fusion.3 = (f32[36,128,128]{2,0,1:T(8,128)}, f32[36,128,128]{2,0,1:T(8,128)}) fusion(s32[]{:T(128)S(6)} %select_n.248, f32[36,128,128]{2,0,1:T(8,128)} %get-tuple-element.22, f32[36,128,128]{2,0,1:T(8,128)} %get-tuple-element.13), kind=kLoop, calls=%fused_computation.75 | loop fusion | flops 1179648 | bytes 9437188 | tf_op jit(solution)/shard_map/jit(_roll_dynamic)/concatenate | solution.py:30
  230.1 4.8 %fusion.24 = (f32[36,128,128]{2,0,1:T(8,128)}, f32[36,128,128]{2,0,1:T(8,128)}) fusion(s32[]{:T(128)S(6)} %select_n.220, f32[36,128,128]{2,0,1:T(8,128)S(1)} %copy-done.15, s32[]{:T(128)S(6)} %select_n.216, f32[36,128,128]{2,0,1:T(8,128)S(1)} %copy-done.14), kind=kLoop, calls=%fused_computation.96 | loop fusion | flops 1179648 | bytes 9437192 | tf_op jit(solution)/shard_map/jit(_roll_dynamic)/concatenate | solution.py:30
  234.9 4.7 %fusion.6 = (f32[36,128,128]{2,0,1:T(8,128)}, f32[36,128,128]{2,0,1:T(8,128)}) fusion(s32[]{:T(128)S(6)} %select_n.244, f32[36,128,128]{2,0,1:T(8,128)S(1)} %copy-done.12, s32[]{:T(128)S(6)} %select_n.240, f32[36,128,128]{2,0,1:T(8,128)S(1)} %copy-done.13), kind=kLoop, calls=%fused_computation.78 | loop fusion | flops 1179648 | bytes 9437192 | tf_op jit(solution)/shard_map/jit(_roll_dynamic)/concatenate | solution.py:30
  239.6 4.6 %fusion.12 = (f32[36,128,128]{2,0,1:T(8,128)}, f32[36,128,128]{2,0,1:T(8,128)}) fusion(s32[]{:T(128)S(6)} %select_n.236, f32[36,128,128]{2,0,1:T(8,128)S(1)} %copy-done.10, s32[]{:T(128)S(6)} %select_n.232, f32[36,128,128]{2,0,1:T(8,128)S(1)} %copy-done.11), kind=kLoop, calls=%fused_computation.84 | loop fusion | flops 1179648 | bytes 9437192 | tf_op jit(solution)/shard_map/jit(_roll_dynamic)/concatenate | solution.py:30
  244.2 4.8 %fusion.18 = (f32[36,128,128]{2,0,1:T(8,128)}, f32[36,128,128]{2,0,1:T(8,128)}) fusion(s32[]{:T(128)S(6)} %select_n.228, f32[36,128,128]{2,0,1:T(8,128)S(1)} %copy-done.8, s32[]{:T(128)S(6)} %select_n.224, f32[36,128,128]{2,0,1:T(8,128)S(1)} %copy-done.9), kind=kLoop, calls=%fused_computation.90 | loop fusion | flops 1179648 | bytes 9437192 | tf_op jit(solution)/shard_map/jit(_roll_dynamic)/concatenate | solution.py:30
  249.0 26.4 %fusion.2 = f32[36,128,128]{2,0,1:T(8,128)S(1)} fusion(s32[]{:T(128)S(6)} %select_n.250, f32[36,128,128]{2,0,1:T(8,128)} %get-tuple-element.74, s32[]{:T(128)S(6)} %select_n.246, f32[36,128,128]{2,0,1:T(8,128)} %get-tuple-element.78, s32[]{:T(128)S(6)} %select_n.242, f32[36,128,128]{2,0,1:T(8,128)} %get-tuple-element.79, s32[]{:T(128)S(6)} %select_n.238, ...), kind=kLoop, calls=%fused_computation.74 | loop fusion | flops 10616832 | bytes 23592996 | tf_op jit(solution)/shard_map/mul | solution.py:62
  276.1 3.0 copy.32
  279.4 6.6 %fusion.51 = (f32[36,128,128]{2,0,1:T(8,128)}, f32[36,128,128]{2,0,1:T(8,128)}) fusion(s32[]{:T(128)S(6)} %select_n.220, f32[36,128,128]{2,0,1:T(8,128)} %get-tuple-element.20, s32[]{:T(128)S(6)} %select_n.216, f32[36,128,128]{2,0,1:T(8,128)} %get-tuple-element.12), kind=kLoop, calls=%fused_computation.123 | loop fusion | flops 1179648 | bytes 9437192 | tf_op jit(solution)/shard_map/jit(_roll_dynamic)/concatenate | solution.py:30
  286.1 4.7 %fusion.33 = (f32[36,128,128]{2,0,1:T(8,128)}, f32[36,128,128]{2,0,1:T(8,128)}) fusion(s32[]{:T(128)S(6)} %select_n.244, f32[36,128,128]{2,0,1:T(8,128)S(1)} %copy-done.6, s32[]{:T(128)S(6)} %select_n.240, f32[36,128,128]{2,0,1:T(8,128)S(1)} %copy-done.7), kind=kLoop, calls=%fused_computation.105 | loop fusion | flops 1179648 | bytes 9437192 | tf_op jit(solution)/shard_map/jit(_roll_dynamic)/concatenate | solution.py:30
  290.8 4.7 %fusion.39 = (f32[36,128,128]{2,0,1:T(8,128)}, f32[36,128,128]{2,0,1:T(8,128)}) fusion(s32[]{:T(128)S(6)} %select_n.236, f32[36,128,128]{2,0,1:T(8,128)S(1)} %copy-done.4, s32[]{:T(128)S(6)} %select_n.232, f32[36,128,128]{2,0,1:T(8,128)S(1)} %copy-done.5), kind=kLoop, calls=%fused_computation.111 | loop fusion | flops 1179648 | bytes 9437192 | tf_op jit(solution)/shard_map/jit(_roll_dynamic)/concatenate | solution.py:30
  295.5 4.8 %fusion.45 = (f32[36,128,128]{2,0,1:T(8,128)}, f32[36,128,128]{2,0,1:T(8,128)}) fusion(s32[]{:T(128)S(6)} %select_n.228, f32[36,128,128]{2,0,1:T(8,128)S(1)} %copy-done.2, s32[]{:T(128)S(6)} %select_n.224, f32[36,128,128]{2,0,1:T(8,128)S(1)} %copy-done.3), kind=kLoop, calls=%fused_computation.117 | loop fusion | flops 1179648 | bytes 9437192 | tf_op jit(solution)/shard_map/jit(_roll_dynamic)/concatenate | solution.py:30
  300.3 25.4 %fusion.29 = f32[36,128,128]{2,0,1:T(8,128)S(1)} fusion(s32[]{:T(128)S(6)} %select_n.250, f32[36,128,128]{2,0,1:T(8,128)} %get-tuple-element.75, s32[]{:T(128)S(6)} %select_n.246, f32[36,128,128]{2,0,1:T(8,128)} %get-tuple-element.86, s32[]{:T(128)S(6)} %select_n.242, f32[36,128,128]{2,0,1:T(8,128)} %get-tuple-element.87, s32[]{:T(128)S(6)} %select_n.238, ...), kind=kLoop, calls=%fused_computation.101 | loop fusion | flops 10616832 | bytes 23592996 | tf_op jit(solution)/shard_map/mul | solution.py:62
  326.5 3.0 copy.29
  330.1 14.9 %reduce-scatter.5.cloned.1.call-done = f32[36,1024]{1,0:T(8,128)} async-done(((f32[36,16384]{1,0:T(8,128)}), f32[36,1024]{1,0:T(8,128)}) %reduce-scatter.5.cloned.1.call-update) | async-done | bytes 147472 | tf_op jit(solution)/shard_map/reduce_scatter | solution.py:66
  345.0 66.6 %reduce-scatter.3.cloned.1.call-done = f32[36,1024]{1,0:T(8,128)} async-done(((f32[36,16384]{1,0:T(8,128)}), f32[36,1024]{1,0:T(8,128)}) %reduce-scatter.3.cloned.1.call-update) | async-done | bytes 147472 | tf_op jit(solution)/shard_map/reduce_scatter | solution.py:66
  (113 shorter events, 36.1 us)
Async XLA Ops:
  7.2 146.5 %copy-start = (bf16[64,16384]{1,0:T(8,128)(2,1)S(1)}, bf16[64,16384]{1,0:T(8,128)(2,1)}, u32[]{:S(2)}) copy-start(bf16[64,16384]{1,0:T(8,128)(2,1)} %param.9) | copy-start | bytes 6291460
  7.2 337.8 %reduce-scatter.5.cloned.1.call-start = ((), (), s32[]{:S(2)}) async-start(), calls=%async_computation.3 | async-start | bytes 2785280 | tf_op jit(solution)/shard_map/reduce_scatter | solution.py:66
  109.2 3.0 copy-start.31
  109.2 4.3 %copy-start.30 = (bf16[36,128,128]{2,1,0:T(8,128)(2,1)S(1)}, bf16[36,128,128]{2,1,0:T(8,128)(2,1)}, u32[]{:S(2)}) copy-start(bf16[36,128,128]{2,1,0:T(8,128)(2,1)} %get-tuple-element.45) | copy-start | bytes 3538948
  112.1 2.7 copy-start.29
  113.5 2.7 copy-start.28
  114.8 2.7 copy-start.27
  116.2 2.7 copy-start.26
  117.5 2.7 copy-start.25
  118.9 2.7 copy-start.24
  124.3 7.9 %copy-start.23 = (bf16[36,128,128]{2,1,0:T(8,128)(2,1)S(1)}, bf16[36,128,128]{2,1,0:T(8,128)(2,1)}, u32[]{:S(2)}) copy-start(bf16[36,128,128]{2,1,0:T(8,128)(2,1)} %get-tuple-element.38) | copy-start | bytes 3538948
  133.2 3.0 copy-start.20
  134.8 2.8 copy-start.19
  136.2 2.7 copy-start.18
  137.5 2.7 copy-start.17
  138.9 2.7 copy-start.16
  224.1 6.0 %copy-start.14 = (f32[36,128,128]{2,0,1:T(8,128)S(1)}, f32[36,128,128]{2,0,1:T(8,128)}, u32[]{:S(2)}) copy-start(f32[36,128,128]{2,0,1:T(8,128)} %get-tuple-element.21) | copy-start | bytes 7077892
  224.1 6.0 %copy-start.15 = (f32[36,128,128]{2,0,1:T(8,128)S(1)}, f32[36,128,128]{2,0,1:T(8,128)}, u32[]{:S(2)}) copy-start(f32[36,128,128]{2,0,1:T(8,128)} %get-tuple-element.29) | copy-start | bytes 7077892
  230.1 4.8 %copy-start.12 = (f32[36,128,128]{2,0,1:T(8,128)S(1)}, f32[36,128,128]{2,0,1:T(8,128)}, u32[]{:S(2)}) copy-start(f32[36,128,128]{2,0,1:T(8,128)} %get-tuple-element.23) | copy-start | bytes 7077892
  230.1 4.8 %copy-start.13 = (f32[36,128,128]{2,0,1:T(8,128)S(1)}, f32[36,128,128]{2,0,1:T(8,128)}, u32[]{:S(2)}) copy-start(f32[36,128,128]{2,0,1:T(8,128)} %get-tuple-element.24) | copy-start | bytes 7077892
  234.9 4.7 %copy-start.10 = (f32[36,128,128]{2,0,1:T(8,128)S(1)}, f32[36,128,128]{2,0,1:T(8,128)}, u32[]{:S(2)}) copy-start(f32[36,128,128]{2,0,1:T(8,128)} %get-tuple-element.25) | copy-start | bytes 7077892
  234.9 4.7 %copy-start.11 = (f32[36,128,128]{2,0,1:T(8,128)S(1)}, f32[36,128,128]{2,0,1:T(8,128)}, u32[]{:S(2)}) copy-start(f32[36,128,128]{2,0,1:T(8,128)} %get-tuple-element.26) | copy-start | bytes 7077892
  239.6 4.7 %copy-start.8 = (f32[36,128,128]{2,0,1:T(8,128)S(1)}, f32[36,128,128]{2,0,1:T(8,128)}, u32[]{:S(2)}) copy-start(f32[36,128,128]{2,0,1:T(8,128)} %get-tuple-element.27) | copy-start | bytes 7077892
  239.6 4.7 %copy-start.9 = (f32[36,128,128]{2,0,1:T(8,128)S(1)}, f32[36,128,128]{2,0,1:T(8,128)}, u32[]{:S(2)}) copy-start(f32[36,128,128]{2,0,1:T(8,128)} %get-tuple-element.28) | copy-start | bytes 7077892
  279.2 132.4 %reduce-scatter.3.cloned.1.call-start = ((), (), s32[]{:S(2)}) async-start(), calls=%async_computation.2 | async-start | bytes 2785280 | tf_op jit(solution)/shard_map/reduce_scatter | solution.py:66
  279.4 6.6 %copy-start.6 = (f32[36,128,128]{2,0,1:T(8,128)S(1)}, f32[36,128,128]{2,0,1:T(8,128)}, u32[]{:S(2)}) copy-start(f32[36,128,128]{2,0,1:T(8,128)} %get-tuple-element.14) | copy-start | bytes 7077892
  279.4 6.6 %copy-start.7 = (f32[36,128,128]{2,0,1:T(8,128)S(1)}, f32[36,128,128]{2,0,1:T(8,128)}, u32[]{:S(2)}) copy-start(f32[36,128,128]{2,0,1:T(8,128)} %get-tuple-element.15) | copy-start | bytes 7077892
  286.0 4.8 %copy-start.4 = (f32[36,128,128]{2,0,1:T(8,128)S(1)}, f32[36,128,128]{2,0,1:T(8,128)}, u32[]{:S(2)}) copy-start(f32[36,128,128]{2,0,1:T(8,128)} %get-tuple-element.16) | copy-start | bytes 7077892
  286.1 4.8 %copy-start.5 = (f32[36,128,128]{2,0,1:T(8,128)S(1)}, f32[36,128,128]{2,0,1:T(8,128)}, u32[]{:S(2)}) copy-start(f32[36,128,128]{2,0,1:T(8,128)} %get-tuple-element.17) | copy-start | bytes 7077892
  290.8 4.7 %copy-start.2 = (f32[36,128,128]{2,0,1:T(8,128)S(1)}, f32[36,128,128]{2,0,1:T(8,128)}, u32[]{:S(2)}) copy-start(f32[36,128,128]{2,0,1:T(8,128)} %get-tuple-element.18) | copy-start | bytes 7077892
  290.8 4.7 %copy-start.3 = (f32[36,128,128]{2,0,1:T(8,128)S(1)}, f32[36,128,128]{2,0,1:T(8,128)}, u32[]{:S(2)}) copy-start(f32[36,128,128]{2,0,1:T(8,128)} %get-tuple-element.19) | copy-start | bytes 7077892
  326.5 87.1 %copy-start.1 = (bf16[64,16384]{1,0:T(8,128)(2,1)S(1)}, bf16[64,16384]{1,0:T(8,128)(2,1)}, u32[]{:S(2)}) copy-start(bf16[64,16384]{1,0:T(8,128)(2,1)} %param.9) | copy-start | bytes 6291460
  (2 other events, 3.9 us)
Sparse Core Ops, SparseCore 0:
  279.3 65.6 reduce-scatter.4
  348.8 62.8 reduce-scatter.2
where the time goes:
time: 426 us; the launch traced here: 421 us
  other arithmetic  125 us (29%)
  local copies, waits for them, and re-layouts  113 us (27%)
  waiting for transfers between devices  81.5 us (19%)
  between operations  64.1 us (15%)
  matrix products  25.8 us (6%)
  blocking collectives  10.8 us (3%)
    reduce_scatter x2, waiting for transfers between devices, per_device(): lax.psum_scatter(partial_sum, 'dat', scatter_dimension=1, tiled=True)  81.5 us
    mul x2, other arithmetic, per_device(): partials.append(align_back(weighted, shift_offsets) * norm_scale)  51.8 us
    concatenate x9, other arithmetic, align_back(): jnp.roll(weighted_grids[:, shift_index], (-shift_offsets[shift_index, 0],...  45.7 us
    squeeze x2, local copies, waits for them, and re-layouts, align_back(): weighted_grids[:, shift_index]  32.7 us
    unnamed x77, local copies, waits for them, and re-layouts  29.8 us
    dynamic_slice x2, local copies, waits for them, and re-layouts, shifted_table(): jnp.roll(images, (shift_offsets[shift_index, 0], shift_offsets[shift_inde...  26.5 us
    unnamed x16, other arithmetic  22.6 us
    dot_general x2, matrix products, per_device(): lax.dot_general(weights, particles, (((0,), (0,)), ((), ())), preferred_e...  19.1 us
  transfers between devices with their start and end apart: 2, of which 2 were waited for; matrix products, arithmetic and copies ran while one was open for 12% of the time, Pallas kernels for 0%

commit v1 on v0

v1 whole, which is shorter than its diff:
```python
import functools
import math

import jax
import jax.numpy as jnp
from jax import lax
from jax.experimental import pallas as pl
from jax.experimental.pallas import tpu as pltpu
from jax.sharding import PartitionSpec as P

SIDE = 128
PIXELS = SIDE * SIDE
CLASSES = 2
ROW_STEP = 4
EDGE = ROW_STEP * SIDE
MESH = pl.DeviceIdType.MESH
FAR = 1e30


def stage_of(slot):
    return (slot & -slot).bit_length() - 1


def kernel(
    n_ref, n_dat, norm_scale,
    order_ref, shift_ref, norm_ref, part_ref, refs_ref,
    sums_ref, evid_ref,
    moved, table, scores, weights, acc, inbox, stats_out, stats_in,
    send_sem, recv_sem, stat_send, stat_recv,
):
    count = part_ref.shape[0]
    rots = refs_ref.shape[1]
    pad = table.shape[0] // CLASSES
    block = acc.shape[2]
    my_ref = lax.axis_index("ref")
    me = lax.axis_index("dat")
    stages = n_dat.bit_length() - 1
    bits = [lax.rem(me // (1 << s), 2) for s in range(stages)]

    def partner(s):
        return me + (1 << s) * (1 - 2 * bits[s])

    barrier = pltpu.get_barrier_semaphore()
    for s in range(stages):
        pl.semaphore_signal(barrier, inc=1, device_id=(my_ref, partner(s)), device_id_type=MESH)
    for o in range(1, n_ref):
        pl.semaphore_signal(
            barrier, inc=1, device_id=(lax.rem(my_ref + o, n_ref), me), device_id_type=MESH
        )

    step = shift_ref[0, 1]
    for k in range(1, shift_ref.shape[0]):
        step = jnp.maximum(step, shift_ref[k, 1])
    source = lax.broadcasted_iota(jnp.int32, (SIDE, SIDE), 0)
    target = lax.broadcasted_iota(jnp.int32, (SIDE, SIDE), 1)
    distance = source - target
    up = jnp.where((distance == step) | (distance == step - SIDE), 1.0, 0.0)
    down = jnp.where((distance == -step) | (distance == SIDE - step), 1.0, 0.0)
    permute = jnp.concatenate([up, down], axis=1).astype(jnp.bfloat16)
    tile_group = 8

    def move(g, carry):
        for j in range(tile_group):
            at = pl.multiple_of((g * tile_group + j) * SIDE, SIDE)
            piece = part_ref[:, pl.ds(at, SIDE)]
            both = jnp.dot(piece, permute, preferred_element_type=jnp.float32).astype(jnp.bfloat16)
            moved[0:count, pl.ds(EDGE + at, SIDE)] = piece
            moved[count : 2 * count, pl.ds(EDGE + at, SIDE)] = both[:, :SIDE]
            moved[2 * count : 3 * count, pl.ds(EDGE + at, SIDE)] = both[:, SIDE:]
        return carry

    lax.fori_loop(0, SIDE // tile_group, move, 0)
    moved[:, 0:EDGE] = moved[:, PIXELS : PIXELS + EDGE]
    moved[:, EDGE + PIXELS : 2 * EDGE + PIXELS] = moved[:, EDGE : 2 * EDGE]

    low = (rots // 16) * 16
    for c in range(CLASSES):
        if low < pad:
            table[c * pad + low : (c + 1) * pad, :] = jnp.zeros(
                (pad - low, table.shape[1]), jnp.bfloat16
            )
        table[c * pad : c * pad + rots, EDGE : EDGE + PIXELS] = refs_ref[c]
    table[:, 0:EDGE] = table[:, PIXELS : PIXELS + EDGE]
    table[:, EDGE + PIXELS : 2 * EDGE + PIXELS] = table[:, EDGE : 2 * EDGE]

    scores[...] = jnp.zeros_like(scores)
    depth = 2048

    def score(g, carry):
        at = pl.multiple_of(g * depth, depth)
        left = jnp.concatenate([table[:, pl.ds(at + a * EDGE, depth)] for a in range(3)], axis=0)
        right = moved[:, pl.ds(EDGE + at, depth)]
        scores[...] += lax.dot_general(
            left, right, (((1,), (1,)), ((), ())), preferred_element_type=jnp.float32
        )
        return carry

    lax.fori_loop(0, PIXELS // depth, score, 0)

    eye = lax.broadcasted_iota(jnp.int32, (rots, rots), 0) == lax.broadcasted_iota(
        jnp.int32, (rots, rots), 1
    )

    def fold(row, op):
        return op(op(row[:, 0:count], row[:, count : 2 * count]), row[:, 2 * count : 3 * count])

    def spread(row):
        return jnp.concatenate([row, row, row], axis=1)

    stats_out[...] = jnp.zeros_like(stats_out)
    exps = []
    highs = []
    totals = []
    for c in range(CLASSES):
        norm_column = jnp.sum(
            jnp.where(eye, norm_ref[c : c + 1, :], 0.0), axis=1, keepdims=True
        )
        parts = [
            scores[(a * CLASSES + c) * pad : (a * CLASSES + c) * pad + rots, :] - norm_column
            for a in range(3)
        ]
        best = jnp.maximum(jnp.maximum(parts[0], parts[1]), parts[2])
        high = fold(jnp.max(best, axis=0, keepdims=True), jnp.maximum)
        wide = spread(high)
        grown = [jnp.exp(p - wide) for p in parts]
        total = fold(jnp.sum(grown[0] + grown[1] + grown[2], axis=0, keepdims=True), jnp.add)
        exps.append(grown)
        highs.append(high)
        totals.append(total)
        stats_out[c : c + 1, 0:count] = high
        stats_out[CLASSES + c : CLASSES + c + 1, 0:count] = total

    pl.semaphore_wait(barrier, stages + n_ref - 1)
    notes = []
    for o in range(1, n_ref):
        note = pltpu.make_async_remote_copy(
            src_ref=stats_out,
            dst_ref=stats_in.at[o - 1],
            send_sem=stat_send.at[o - 1],
            recv_sem=stat_recv.at[o - 1],
            device_id=(lax.rem(my_ref + o, n_ref), me),
            device_id_type=MESH,
        )
        note.start()
        notes.append(note)
    for note in notes:
        note.wait()

    first = order_ref[0] == 0
    finals = []
    evidence = []
    for c in range(CLASSES):
        high = highs[c]
        for o in range(1, n_ref):
            high = jnp.maximum(high, stats_in[o - 1, c : c + 1, 0:count])
        mine = jnp.exp(highs[c] - high)
        total = totals[c] * mine
        for o in range(1, n_ref):
            total = total + stats_in[o - 1, CLASSES + c : CLASSES + c + 1, 0:count] * jnp.exp(
                stats_in[o - 1, c : c + 1, 0:count] - high
            )
        factor = spread(mine / total)
        finals.append([e * factor for e in exps[c]])
        evidence.append(high + jnp.log(total))
    evid_ref[0:1, :] = jnp.where(first, evidence[0], evidence[1])
    evid_ref[1:2, :] = jnp.where(first, evidence[1], evidence[0])
    width = 3 * count
    for a in range(3):
        one, two = finals[0][a], finals[1][a]
        ordered = jnp.concatenate(
            [jnp.where(first, one, two), jnp.where(first, two, one)], axis=0
        )
        weights[a] = ordered.astype(jnp.bfloat16)

    def compute(slot):
        owner = me
        for s in range(stages):
            if (slot >> s) & 1:
                owner = owner + (1 << s) * (1 - 2 * bits[s])
        at = pl.multiple_of(owner * block, block)
        total = jnp.dot(
            weights[0], moved[:, pl.ds(at + 2 * EDGE, block)], preferred_element_type=jnp.float32
        )
        total = total + jnp.dot(
            weights[1], moved[:, pl.ds(at + EDGE, block)], preferred_element_type=jnp.float32
        )
        acc[slot] = total + jnp.dot(
            weights[2], moved[:, pl.ds(at, block)], preferred_element_type=jnp.float32
        )

    copies = {}
    missing = {slot: stage_of(slot) if slot else stages for slot in range(n_dat)}

    def send(slot):
        s = stage_of(slot)
        copies[slot] = pltpu.make_async_remote_copy(
            src_ref=acc.at[slot],
            dst_ref=inbox.at[slot],
            send_sem=send_sem.at[slot],
            recv_sem=recv_sem.at[slot],
            device_id=(my_ref, partner(s)),
            device_id_type=MESH,
        )
        copies[slot].start()

    def finish(slot):
        into = slot & (slot - 1)
        copies[slot].wait_recv()
        acc[into] = acc[into] + inbox[slot]
        missing[into] -= 1
        if into and missing[into] == 0:
            send(into)

    odd = sorted(range(1, n_dat, 2), key=lambda slot: (-(slot & 2), -slot))
    for place, slot in enumerate(odd):
        compute(slot)
        send(slot)
        compute(slot - 1)
        if place:
            finish(odd[place - 1])
    finish(odd[-1])
    rest = sorted(
        range(2, n_dat, 2), key=lambda slot: (slot <= n_dat // 2, stage_of(slot), -slot)
    )
    for slot in rest:
        finish(slot)
    for slot in range(1, n_dat):
        copies[slot].wait_send()
    for c in range(CLASSES):
        sums_ref[c] = acc[0, c * rots : (c + 1) * rots, :] * norm_scale


def per_device(n_ref, n_dat, particles, references, normalizers, class_order, shift_offsets):
    count = particles.shape[0]
    rots = references.shape[1]
    block = PIXELS // n_dat
    pad = -(-rots // 16) * 16
    rows = CLASSES * rots
    norm_scale = float(rots * n_ref) / math.sqrt(count * n_dat)
    smem = pl.BlockSpec(memory_space=pltpu.SMEM)
    vmem = pl.BlockSpec(memory_space=pltpu.VMEM)
    return pl.pallas_call(
        functools.partial(kernel, n_ref, n_dat, norm_scale),
        out_shape=(
            jax.ShapeDtypeStruct((CLASSES, rots, block), jnp.float32),
            jax.ShapeDtypeStruct((CLASSES, count), jnp.float32),
        ),
        in_specs=[smem, smem, vmem, vmem, vmem],
        out_specs=(vmem, vmem),
        scratch_shapes=[
            pltpu.VMEM((3 * count, PIXELS + 2 * EDGE), jnp.bfloat16),
            pltpu.VMEM((CLASSES * pad, PIXELS + 2 * EDGE), jnp.bfloat16),
            pltpu.VMEM((3 * CLASSES * pad, 3 * count), jnp.float32),
            pltpu.VMEM((3, rows, 3 * count), jnp.bfloat16),
            pltpu.VMEM((n_dat, rows, block), jnp.float32),
            pltpu.VMEM((n_dat, rows, block), jnp.float32),
            pltpu.VMEM((8, 128), jnp.float32),
            pltpu.VMEM((max(n_ref - 1, 1), 8, 128), jnp.float32),
            pltpu.SemaphoreType.DMA((n_dat,)),
            pltpu.SemaphoreType.DMA((n_dat,)),
            pltpu.SemaphoreType.DMA((max(n_ref - 1, 1),)),
            pltpu.SemaphoreType.DMA((max(n_ref - 1, 1),)),
        ],
        compiler_params=pltpu.CompilerParams(
            collective_id=0, has_side_effects=True, vmem_limit_bytes=48 * 1024 * 1024
        ),
    )(class_order, shift_offsets, normalizers, particles, references)


def solution(mesh):
    return jax.shard_map(
        functools.partial(per_device, mesh.shape["ref"], mesh.shape["dat"]),
        mesh=mesh,
        in_specs=(P("dat", None), P(None, "ref", None), P(None, "ref"), P(), P()),
        out_specs=(P(None, "ref", "dat"), P(None, "dat")),
        check_vma=False,
    )
```

time: 426 us -> 58.8 us (0.14); the launches traced: 421 us -> 58.6 us
  other arithmetic: 125 us -> 0 us
  local copies, waits for them, and re-layouts: 113 us -> 5.41 us
  waiting for transfers between devices: 81.5 us -> 0 us
  between operations: 64.1 us -> 0.67 us
  Pallas kernels: 0 us -> 52.5 us
  matrix products: 25.8 us -> 0 us
  blocking collectives: 10.8 us -> 0 us
    reduce_scatter x2 -> x0, waiting for transfers between devices: 81.5 us -> none  [per_device(): lax.psum_scatter(partial_sum, 'dat', scatter_dimension=1, tiled=True)]
    pallas_call x0 -> x1, Pallas kernels: none -> 52.5 us  [per_device(): pl.pallas_call(functools.partial(kernel, n_ref, n_dat, norm_scale), out_s...]
    mul x2 -> x0, other arithmetic: 51.8 us -> none  [per_device(): partials.append(align_back(weighted, shift_offsets) * norm_scale)]
    concatenate x9 -> x0, other arithmetic: 45.7 us -> none  [align_back(): jnp.roll(weighted_grids[:, shift_index], (-shift_offsets[shift_index, 0],...]
    dynamic_slice x3 -> x0, local copies, waits for them, and re-layouts: 42.4 us -> none  [the longest x2 26.5 us: shifted_table(): jnp.roll(images, (shift_offsets[shift_index, 0], shift_offsets[shift_inde...]
    squeeze x2 -> x0, local copies, waits for them, and re-layouts: 32.7 us -> none  [align_back(): weighted_grids[:, shift_index]]
    dot_general x4 -> x0, matrix products: 25.8 us -> none  [the longest x2 19.1 us: per_device(): lax.dot_general(weights, particles, (((0,), (0,)), ((), ())), preferred_e...]
    unnamed x77 -> x9, local copies, waits for them, and re-layouts: 29.8 us -> 4.46 us
  transfers between devices with their start and end apart: 2 -> 0, of which waited for: 2 -> 0; matrix products, arithmetic and copies ran while one was open for 12% -> 0% of each run, Pallas kernels for 0% -> 0%
where the time goes in v1:
time: 58.8 us; the launch traced here: 58.6 us
  Pallas kernels  52.5 us (89%)
  local copies, waits for them, and re-layouts  5.41 us (9%)
  between operations  0.67 us (1%)
    pallas_call x1, Pallas kernels, per_device(): pl.pallas_call(functools.partial(kernel, n_ref, n_dat, norm_scale), out_s...  52.5 us
    unnamed x9, local copies, waits for them, and re-layouts  4.46 us

profile of v1, /device:TPU:0, one launch (start us, length us, event | category | flops | bytes accessed | tf_op | source)
XLA Modules:
  0.0 58.6 jit_solution(2756926806545197512)
XLA Ops:
  0.6 0.8 %copy.7.shift_ref = s32[9,2]{1,0:T(8,128)S(1)} copy(s32[9,2]{0,1:T(2,128)} %param.9) | data formatting | bytes 144 | tf_op args[4]
  1.4 0.0 copy-start
  1.4 0.0 copy-start.1
  1.4 0.0 copy-start.2
  1.4 3.1 %copy.8.refs_ref = bf16[2,36,16384]{2,1,0:T(8,128)(2,1)S(1)} copy(bf16[2,36,16384]{2,0,1:T(2,128)(2,1)} %param.6) | data formatting | bytes 4718592 | tf_op args[1]
  4.5 0.0 copy-done
  4.5 0.0 copy-done.1
  4.6 0.0 copy-done.2
  4.6 52.5 %shard_map.68 = (f32[2,36,1024]{2,1,0:T(8,128)S(1)}, f32[2,64]{1,0:T(2,128)S(1)}) custom-call(s32[2]{0:T(128)S(1)} %copy-done.2, s32[9,2]{1,0:T(8,128)S(1)} %copy.7.shift_ref, f32[2,36]{1,0:T(2,128)S(1)} %copy-done.1, bf16[64,16384]{1,0:T(8,128)(2,1)S(1)} %copy-done, bf16[2,36,16384]{2,1,0:T(8,128)(2,1)S(1)} %copy.8.refs_ref), custom_call_target="tpu_custom_call" | custom-call | tf_op jit(solution)/shard_map/pallas_call | solution.py:242
  57.1 0.9 %copy.9 = f32[2,36,1024]{2,0,1:T(2,128)} copy(f32[2,36,1024]{2,1,0:T(8,128)S(1)} %get-tuple-element.2) | data formatting | bytes 589824 | tf_op jit(solution)/shard_map/pallas_call | solution.py:242
  58.0 0.6 copy.11
Async XLA Ops:
  1.4 3.1 %copy-start = (bf16[64,16384]{1,0:T(8,128)(2,1)S(1)}, bf16[64,16384]{1,0:T(8,128)(2,1)}, u32[]{:S(2)}) copy-start(bf16[64,16384]{1,0:T(8,128)(2,1)} %part_ref.1) | copy-start | bytes 6291460
  1.4 3.1 %copy-start.1 = (f32[2,36]{1,0:T(2,128)S(1)}, f32[2,36]{1,0:T(2,128)}, u32[]{:S(2)}) copy-start(f32[2,36]{1,0:T(2,128)} %norm_ref.1) | copy-start | bytes 868
  1.4 3.2 %copy-start.2 = (s32[2]{0:T(128)S(1)}, s32[2]{0:T(128)}, u32[]{:S(2)}) copy-start(s32[2]{0:T(128)} %order_ref.1) | copy-start | bytes 28

commit v2 on v1

v2 whole, which is shorter than its diff:
```python
import functools
import math

import jax
import jax.numpy as jnp
from jax import lax
from jax.experimental import pallas as pl
from jax.experimental.pallas import tpu as pltpu
from jax.sharding import PartitionSpec as P

SIDE = 128
PIXELS = SIDE * SIDE
CLASSES = 2
ROW_STEP = 4
EDGE = ROW_STEP * SIDE
MESH = pl.DeviceIdType.MESH


def stage_of(slot):
    return (slot & -slot).bit_length() - 1


def whole_plan(n):
    plan = []
    for t in range(CLASSES):
        if t:
            plan += [("score", t, 0), ("weigh", t, 0)]
        odd = range(n - 1, 0, -2)
        for slot in odd:
            plan += [("calc", t, slot), ("calc", t, slot - 1)]
        plan += [("take", t, slot) for slot in odd]
    rest = sorted(range(2, n, 2), key=lambda slot: (stage_of(slot), -slot))
    return plan + [("take", t, slot) for slot in rest for t in range(CLASSES)]


PLAN16 = (
    ("c", 0, 15), ("c", 0, 14), ("c", 0, 11), ("t", 0, 15), ("c", 0, 10), ("c", 0, 7),
    ("t", 0, 11), ("c", 0, 6), ("c", 0, 13), ("t", 0, 7), ("c", 0, 12), ("c", 0, 9),
    ("c", 0, 8), ("c", 0, 5), ("c", 0, 4), ("t", 0, 13), ("t", 0, 9), ("t", 0, 5),
    ("s", 1, 0), ("t", 0, 14), ("c", 0, 3), ("c", 0, 2), ("c", 0, 1), ("c", 0, 0),
    ("t", 0, 1), ("w", 1, 0),
    ("c", 1, 15), ("c", 1, 14), ("c", 1, 11), ("t", 1, 15), ("c", 1, 10), ("c", 1, 7),
    ("t", 1, 11), ("c", 1, 6), ("c", 1, 3), ("t", 1, 7), ("t", 0, 3), ("t", 0, 10),
    ("t", 0, 12),
    ("c", 1, 2), ("c", 1, 13), ("c", 1, 12), ("t", 1, 3), ("c", 1, 9), ("c", 1, 8),
    ("t", 1, 13), ("t", 0, 6), ("c", 1, 5), ("c", 1, 4), ("t", 1, 9), ("c", 1, 1),
    ("c", 1, 0), ("t", 1, 1),
    ("t", 1, 6), ("t", 1, 14), ("t", 1, 5), ("t", 1, 10), ("t", 1, 12), ("t", 0, 2),
    ("t", 0, 4), ("t", 0, 8), ("t", 1, 4), ("t", 1, 2), ("t", 1, 8),
)


def plan_of(n):
    if n != 16:
        return whole_plan(n), {}
    names = {"c": "calc", "t": "take", "s": "score", "w": "weigh"}
    steps = [(names[kind], t, slot) for kind, t, slot in PLAN16]
    return steps, {(1, 6): (2, 2)}


def kernel(
    n_ref, n_dat, norm_scale,
    order_ref, shift_ref, norm_ref, part_ref, refs_ref,
    sums_ref, evid_ref,
    moved, table, scores, grown, weights, acc, inbox, stats_out, stats_in,
    send_sem, recv_sem, stat_send, stat_recv,
):
    count = part_ref.shape[0]
    rots = refs_ref.shape[1]
    pad = table.shape[0]
    block = acc.shape[3]
    my_ref = lax.axis_index("ref")
    me = lax.axis_index("dat")
    stages = n_dat.bit_length() - 1
    bits = [lax.rem(me // (1 << s), 2) for s in range(stages)]

    def partner(s):
        return me + (1 << s) * (1 - 2 * bits[s])

    barrier = pltpu.get_barrier_semaphore()
    for s in range(stages):
        pl.semaphore_signal(barrier, inc=1, device_id=(my_ref, partner(s)), device_id_type=MESH)
    for o in range(1, n_ref):
        pl.semaphore_signal(
            barrier, inc=1, device_id=(lax.rem(my_ref + o, n_ref), me), device_id_type=MESH
        )

    step = shift_ref[1, 0]
    for k in range(1, shift_ref.shape[1]):
        step = jnp.maximum(step, shift_ref[1, k])
    source = lax.broadcasted_iota(jnp.int32, (SIDE, SIDE), 0)
    target = lax.broadcasted_iota(jnp.int32, (SIDE, SIDE), 1)
    distance = source - target
    up = jnp.where((distance == step) | (distance == step - SIDE), 1.0, 0.0)
    down = jnp.where((distance == -step) | (distance == SIDE - step), 1.0, 0.0)
    permute = jnp.concatenate([up, down], axis=1).astype(jnp.bfloat16)
    tile_group = 8

    def move(g, carry):
        for j in range(tile_group):
            at = pl.multiple_of((g * tile_group + j) * SIDE, SIDE)
            piece = part_ref[:, pl.ds(at, SIDE)]
            both = jnp.dot(piece, permute, preferred_element_type=jnp.float32).astype(jnp.bfloat16)
            moved[0:count, pl.ds(EDGE + at, SIDE)] = piece
            moved[count : 2 * count, pl.ds(EDGE + at, SIDE)] = both[:, :SIDE]
            moved[2 * count : 3 * count, pl.ds(EDGE + at, SIDE)] = both[:, SIDE:]
        return carry

    lax.fori_loop(0, SIDE // tile_group, move, 0)
    moved[:, 0:EDGE] = moved[:, PIXELS : PIXELS + EDGE]
    moved[:, EDGE + PIXELS : 2 * EDGE + PIXELS] = moved[:, EDGE : 2 * EDGE]

    low = (rots // 16) * 16
    depth = 2048
    eye = lax.broadcasted_iota(jnp.int32, (rots, rots), 0) == lax.broadcasted_iota(
        jnp.int32, (rots, rots), 1
    )

    def fold(row, op):
        return op(op(row[:, 0:count], row[:, count : 2 * count]), row[:, 2 * count : 3 * count])

    def spread(row):
        return jnp.concatenate([row, row, row], axis=1)

    def score_step(t):
        chosen = order_ref[t]
        if low < pad:
            table[low:pad, :] = jnp.zeros((pad - low, table.shape[1]), jnp.bfloat16)
        table[0:rots, EDGE : EDGE + PIXELS] = refs_ref[chosen]
        table[:, 0:EDGE] = table[:, PIXELS : PIXELS + EDGE]
        table[:, EDGE + PIXELS : 2 * EDGE + PIXELS] = table[:, EDGE : 2 * EDGE]

        scores[...] = jnp.zeros_like(scores)

        def score(g, carry):
            at = pl.multiple_of(g * depth, depth)
            left = jnp.concatenate(
                [table[:, pl.ds(at + a * EDGE, depth)] for a in range(3)], axis=0
            )
            right = moved[:, pl.ds(EDGE + at, depth)]
            scores[...] += lax.dot_general(
                left, right, (((1,), (1,)), ((), ())), preferred_element_type=jnp.float32
            )
            return carry

        lax.fori_loop(0, PIXELS // depth, score, 0)
        columns = [
            jnp.sum(jnp.where(eye, norm_ref[c : c + 1, :], 0.0), axis=1, keepdims=True)
            for c in range(CLASSES)
        ]
        norm_column = jnp.where(chosen == 0, columns[0], columns[1])
        parts = [scores[a * pad : a * pad + rots, :] - norm_column for a in range(3)]
        best = jnp.maximum(jnp.maximum(parts[0], parts[1]), parts[2])
        high = fold(jnp.max(best, axis=0, keepdims=True), jnp.maximum)
        wide = spread(high)
        raised = [jnp.exp(p - wide) for p in parts]
        total = fold(jnp.sum(raised[0] + raised[1] + raised[2], axis=0, keepdims=True), jnp.add)
        for a in range(3):
            grown[a] = raised[a]
        stats_out[t] = jnp.zeros((8, 128), jnp.float32)
        stats_out[t, 0:1, 0:count] = high
        stats_out[t, 1:2, 0:count] = total
        if t == 0:
            pl.semaphore_wait(barrier, stages + n_ref - 1)
        notes = []
        for o in range(1, n_ref):
            note = pltpu.make_async_remote_copy(
                src_ref=stats_out.at[t],
                dst_ref=stats_in.at[t, o - 1],
                send_sem=stat_send.at[t, o - 1],
                recv_sem=stat_recv.at[t, o - 1],
                device_id=(lax.rem(my_ref + o, n_ref), me),
                device_id_type=MESH,
            )
            note.start()
            notes.append(note)
        return notes

    def weigh_step(t, notes):
        for note in notes:
            note.wait()
        own = stats_out[t, 0:1, 0:count]
        high = own
        for o in range(1, n_ref):
            high = jnp.maximum(high, stats_in[t, o - 1, 0:1, 0:count])
        mine = jnp.exp(own - high)
        total = stats_out[t, 1:2, 0:count] * mine
        for o in range(1, n_ref):
            total = total + stats_in[t, o - 1, 1:2, 0:count] * jnp.exp(
                stats_in[t, o - 1, 0:1, 0:count] - high
            )
        factor = spread(mine / total)
        for a in range(3):
            weights[t, a] = (grown[a] * factor).astype(jnp.bfloat16)
        evid_ref[t : t + 1, :] = high + jnp.log(total)

    def compute(t, slot):
        owner = me
        for s in range(stages):
            if (slot >> s) & 1:
                owner = owner + (1 << s) * (1 - 2 * bits[s])
        at = pl.multiple_of(owner * block, block)
        total = jnp.dot(
            weights[t, 0], moved[:, pl.ds(at + 2 * EDGE, block)],
            preferred_element_type=jnp.float32,
        )
        total = total + jnp.dot(
            weights[t, 1], moved[:, pl.ds(at + EDGE, block)], preferred_element_type=jnp.float32
        )
        acc[t, slot] = total + jnp.dot(
            weights[t, 2], moved[:, pl.ds(at, block)], preferred_element_type=jnp.float32
        )

    plan, routes = plan_of(n_dat)
    pairs = [(t, slot) for t in range(CLASSES) for slot in range(n_dat)]
    route = {
        (t, slot): routes.get((t, slot), (stage_of(slot), slot & (slot - 1)))
        for t, slot in pairs
        if slot
    }
    missing = {pair: 1 for pair in pairs}
    for (t, slot), (stage, into) in route.items():
        missing[t, into] += 1
    copies = {}

    def ready(t, slot):
        missing[t, slot] -= 1
        if slot == 0 or missing[t, slot]:
            return
        copies[t, slot] = pltpu.make_async_remote_copy(
            src_ref=acc.at[t, slot],
            dst_ref=inbox.at[t, slot],
            send_sem=send_sem.at[t, slot],
            recv_sem=recv_sem.at[t, slot],
            device_id=(my_ref, partner(route[t, slot][0])),
            device_id_type=MESH,
        )
        copies[t, slot].start()

    weigh_step(0, score_step(0))
    notes = None
    for kind, t, slot in plan:
        if kind == "score":
            notes = score_step(t)
        elif kind == "weigh":
            weigh_step(t, notes)
        elif kind == "calc":
            compute(t, slot)
            ready(t, slot)
        else:
            into = route[t, slot][1]
            copies[t, slot].wait_recv()
            acc[t, into] = acc[t, into] + inbox[t, slot]
            ready(t, into)
    for pair in route:
        copies[pair].wait_send()
    for t in range(CLASSES):
        sums_ref[t] = acc[t, 0] * norm_scale


def per_device(n_ref, n_dat, particles, references, normalizers, class_order, shift_offsets):
    count = particles.shape[0]
    rots = references.shape[1]
    block = PIXELS // n_dat
    pad = -(-rots // 16) * 16
    norm_scale = float(rots * n_ref) / math.sqrt(count * n_dat)
    smem = pl.BlockSpec(memory_space=pltpu.SMEM)
    vmem = pl.BlockSpec(memory_space=pltpu.VMEM)
    return pl.pallas_call(
        functools.partial(kernel, n_ref, n_dat, norm_scale),
        out_shape=(
            jax.ShapeDtypeStruct((CLASSES, rots, block), jnp.float32),
            jax.ShapeDtypeStruct((CLASSES, count), jnp.float32),
        ),
        in_specs=[smem, smem, vmem, vmem, vmem],
        out_specs=(vmem, vmem),
        scratch_shapes=[
            pltpu.VMEM((3 * count, PIXELS + 2 * EDGE), jnp.bfloat16),
            pltpu.VMEM((pad, PIXELS + 2 * EDGE), jnp.bfloat16),
            pltpu.VMEM((3 * pad, 3 * count), jnp.float32),
            pltpu.VMEM((3, rots, 3 * count), jnp.float32),
            pltpu.VMEM((CLASSES, 3, rots, 3 * count), jnp.bfloat16),
            pltpu.VMEM((CLASSES, n_dat, rots, block), jnp.float32),
            pltpu.VMEM((CLASSES, n_dat, rots, block), jnp.float32),
            pltpu.VMEM((CLASSES, 8, 128), jnp.float32),
            pltpu.VMEM((CLASSES, max(n_ref - 1, 1), 8, 128), jnp.float32),
            pltpu.SemaphoreType.DMA((CLASSES, n_dat)),
            pltpu.SemaphoreType.DMA((CLASSES, n_dat)),
            pltpu.SemaphoreType.DMA((CLASSES, max(n_ref - 1, 1))),
            pltpu.SemaphoreType.DMA((CLASSES, max(n_ref - 1, 1))),
        ],
        compiler_params=pltpu.CompilerParams(
            collective_id=0, has_side_effects=True, vmem_limit_bytes=48 * 1024 * 1024
        ),
    )(class_order, shift_offsets.T, normalizers, particles, references)


def solution(mesh):
    return jax.shard_map(
        functools.partial(per_device, mesh.shape["ref"], mesh.shape["dat"]),
        mesh=mesh,
        in_specs=(P("dat", None), P(None, "ref", None), P(None, "ref"), P(), P()),
        out_specs=(P(None, "ref", "dat"), P(None, "dat")),
        check_vma=False,
    )
```

time: 58.8 us -> 59.9 us (1.019)
  Pallas kernels: 52.5 us -> 54.4 us
  local copies, waits for them, and re-layouts: 5.41 us -> 4.64 us
    pallas_call x1, Pallas kernels: 52.5 us -> 54.4 us  [per_device(): pl.pallas_call(functools.partial(kernel, n_ref, n_dat, norm_scale), out_s...]
    unnamed x9 -> x10, local copies, waits for them, and re-layouts: 4.46 us -> 3.7 us
where the time goes in v2:
time: 59.9 us; the launch traced here: 59.7 us
  Pallas kernels  54.4 us (91%)
  local copies, waits for them, and re-layouts  4.64 us (8%)
  between operations  0.71 us (1%)
    pallas_call x1, Pallas kernels, per_device(): pl.pallas_call(functools.partial(kernel, n_ref, n_dat, norm_scale), out_s...  54.4 us
    unnamed x10, local copies, waits for them, and re-layouts  3.7 us

profile of v2, /device:TPU:0, one launch (start us, length us, event | category | flops | bytes accessed | tf_op | source)
XLA Modules:
  0.0 59.7 jit_solution(12128079667825053831)
XLA Ops:
  0.6 0.0 copy-start
  0.6 0.0 copy-start.1
  0.7 0.0 copy-start.2
  0.7 0.0 copy-start.3
  0.7 3.1 %copy.7.refs_ref = bf16[2,36,16384]{2,1,0:T(8,128)(2,1)S(1)} copy(bf16[2,36,16384]{2,0,1:T(2,128)(2,1)} %param.6) | data formatting | bytes 4718592 | tf_op args[1]
  3.8 0.0 copy-done
  3.8 0.0 copy-done.1
  3.8 0.0 copy-done.2
  3.8 0.0 copy-done.3
  3.8 54.4 %shard_map.68 = (f32[2,36,1024]{2,1,0:T(8,128)S(1)}, f32[2,64]{1,0:T(2,128)S(1)}) custom-call(s32[2]{0:T(128)S(1)} %copy-done.3, s32[2,9]{1,0:T(2,128)S(1)} %bitcast.1, f32[2,36]{1,0:T(2,128)S(1)} %copy-done.2, bf16[64,16384]{1,0:T(8,128)(2,1)S(1)} %copy-done, bf16[2,36,16384]{2,1,0:T(8,128)(2,1)S(1)} %copy.7.refs_ref), custom_call_target="tpu_custom_call" | custom-call | tf_op jit(solution)/shard_map/pallas_call | solution.py:269
  58.2 0.9 %copy.8 = f32[2,36,1024]{2,0,1:T(2,128)} copy(f32[2,36,1024]{2,1,0:T(8,128)S(1)} %get-tuple-element.2) | data formatting | bytes 589824 | tf_op jit(solution)/shard_map/pallas_call | solution.py:269
  59.2 0.6 copy.10
Async XLA Ops:
  0.6 3.2 %copy-start = (bf16[64,16384]{1,0:T(8,128)(2,1)S(1)}, bf16[64,16384]{1,0:T(8,128)(2,1)}, u32[]{:S(2)}) copy-start(bf16[64,16384]{1,0:T(8,128)(2,1)} %part_ref.1) | copy-start | bytes 6291460
  0.6 3.2 %copy-start.1 = (s32[9,2]{0,1:T(2,128)S(1)}, s32[9,2]{0,1:T(2,128)}, u32[]{:S(2)}) copy-start(s32[9,2]{0,1:T(2,128)} %param.9) | copy-start | bytes 220
  0.7 3.2 %copy-start.2 = (f32[2,36]{1,0:T(2,128)S(1)}, f32[2,36]{1,0:T(2,128)}, u32[]{:S(2)}) copy-start(f32[2,36]{1,0:T(2,128)} %norm_ref.1) | copy-start | bytes 868
  0.7 3.2 %copy-start.3 = (s32[2]{0:T(128)S(1)}, s32[2]{0:T(128)}, u32[]{:S(2)}) copy-start(s32[2]{0:T(128)} %order_ref.1) | copy-start | bytes 28

commit v3 on v1

--- a/solution.py
+++ b/solution.py
@@ -14,7 +14,6 @@
 ROW_STEP = 4
 EDGE = ROW_STEP * SIDE
 MESH = pl.DeviceIdType.MESH
-FAR = 1e30
 
 
 def stage_of(slot):
@@ -48,9 +47,9 @@
             barrier, inc=1, device_id=(lax.rem(my_ref + o, n_ref), me), device_id_type=MESH
         )
 
-    step = shift_ref[0, 1]
-    for k in range(1, shift_ref.shape[0]):
-        step = jnp.maximum(step, shift_ref[k, 1])
+    step = shift_ref[1, 0]
+    for k in range(1, shift_ref.shape[1]):
+        step = jnp.maximum(step, shift_ref[1, k])
     source = lax.broadcasted_iota(jnp.int32, (SIDE, SIDE), 0)
     target = lax.broadcasted_iota(jnp.int32, (SIDE, SIDE), 1)
     distance = source - target
@@ -264,7 +263,7 @@
         compiler_params=pltpu.CompilerParams(
             collective_id=0, has_side_effects=True, vmem_limit_bytes=48 * 1024 * 1024
         ),
-    )(class_order, shift_offsets, normalizers, particles, references)
+    )(class_order, shift_offsets.T, normalizers, particles, references)
 
 
 def solution(mesh):

time: 58.8 us -> 57.9 us (0.985)
  local copies, waits for them, and re-layouts: 5.41 us -> 4.64 us
    unnamed x9 -> x10, local copies, waits for them, and re-layouts: 4.46 us -> 3.7 us
where the time goes in v3:
time: 57.9 us; the launch traced here: 57.8 us
  Pallas kernels  52.4 us (91%)
  local copies, waits for them, and re-layouts  4.64 us (8%)
  between operations  0.71 us (1%)
    pallas_call x1, Pallas kernels, per_device(): pl.pallas_call(functools.partial(kernel, n_ref, n_dat, norm_scale), out_s...  52.4 us
    unnamed x10, local copies, waits for them, and re-layouts  3.7 us

profile of v3, /device:TPU:0, one launch (start us, length us, event | category | flops | bytes accessed | tf_op | source)
XLA Modules:
  0.0 57.8 jit_solution(12635075719778748734)
XLA Ops:
  0.6 0.0 copy-start
  0.6 0.0 copy-start.1
  0.7 0.0 copy-start.2
  0.7 0.0 copy-start.3
  0.7 3.1 %copy.7.refs_ref = bf16[2,36,16384]{2,1,0:T(8,128)(2,1)S(1)} copy(bf16[2,36,16384]{2,0,1:T(2,128)(2,1)} %param.6) | data formatting | bytes 4718592 | tf_op args[1]
  3.8 0.0 copy-done
  3.8 0.0 copy-done.1
  3.8 0.0 copy-done.2
  3.8 0.0 copy-done.3
  3.8 52.4 %shard_map.68 = (f32[2,36,1024]{2,1,0:T(8,128)S(1)}, f32[2,64]{1,0:T(2,128)S(1)}) custom-call(s32[2]{0:T(128)S(1)} %copy-done.3, s32[2,9]{1,0:T(2,128)S(1)} %bitcast.1, f32[2,36]{1,0:T(2,128)S(1)} %copy-done.2, bf16[64,16384]{1,0:T(8,128)(2,1)S(1)} %copy-done, bf16[2,36,16384]{2,1,0:T(8,128)(2,1)S(1)} %copy.7.refs_ref), custom_call_target="tpu_custom_call" | custom-call | tf_op jit(solution)/shard_map/pallas_call | solution.py:241
  56.3 0.9 %copy.8 = f32[2,36,1024]{2,0,1:T(2,128)} copy(f32[2,36,1024]{2,1,0:T(8,128)S(1)} %get-tuple-element.2) | data formatting | bytes 589824 | tf_op jit(solution)/shard_map/pallas_call | solution.py:241
  57.2 0.6 copy.10
Async XLA Ops:
  0.6 3.2 %copy-start = (bf16[64,16384]{1,0:T(8,128)(2,1)S(1)}, bf16[64,16384]{1,0:T(8,128)(2,1)}, u32[]{:S(2)}) copy-start(bf16[64,16384]{1,0:T(8,128)(2,1)} %part_ref.1) | copy-start | bytes 6291460
  0.6 3.2 %copy-start.1 = (s32[9,2]{0,1:T(2,128)S(1)}, s32[9,2]{0,1:T(2,128)}, u32[]{:S(2)}) copy-start(s32[9,2]{0,1:T(2,128)} %param.9) | copy-start | bytes 220
  0.7 3.2 %copy-start.2 = (f32[2,36]{1,0:T(2,128)S(1)}, f32[2,36]{1,0:T(2,128)}, u32[]{:S(2)}) copy-start(f32[2,36]{1,0:T(2,128)} %norm_ref.1) | copy-start | bytes 868
  0.7 3.2 %copy-start.3 = (s32[2]{0:T(128)S(1)}, s32[2]{0:T(128)}, u32[]{:S(2)}) copy-start(s32[2]{0:T(128)} %order_ref.1) | copy-start | bytes 28
